TPU v7x, 256 devices: a whole 4x4x8 slice. The times are simulated.
256 devices in a mesh: blk: 64 (over z_lo, x, y, core), grp: 4 (over z_hi).
Axes of the slice: x: 4, y: 4, z: 8 (z_hi: 4, z_lo: 2; z = z_hi * 2 + z_lo), core: 2. Of those that a mesh axis runs over, the one named last changes fastest.
Arguments:
- queries: bfloat16 [65536, 4096], P(('blk', 'grp')), may hold values from -1 to 1
- documents: bfloat16 [65536, 4096], P(('blk', 'grp')), may hold values from -1 to 1
- positives: int32 [256, 256], P(('blk', 'grp')), may hold values from 0 to 255, as said below
Outputs:
- query_grad: float32 [65536, 4096], P(('blk', 'grp'))
- doc_grad: float32 [65536, 4096], P(('blk', 'grp'))
- loss: float32 [], replicated
Inputs may be any that keep to these rules, and one draw needn't show every extreme that they name: `positives`: each block of 256 rows names each of 0 to 255 exactly once.
All inputs are finite; a program needn't handle non-finite values.
Results may differ from a plain program's by a relative error of at most 0.0036.
Values may be sent and summed in bfloat16 or wider, within the bound.
No kernel may reach another device: no remote copies, remote signals or barrier semaphores. Data moves between devices by JAX's collectives and lax.ppermute only.
A program may use at most 128 MiB of HBM per device.

v0:
```python
import functools

import jax
import jax.numpy as jnp
from jax import lax
from jax.sharding import Mesh
from jax.sharding import PartitionSpec as P

BLK = ("blk_0", "blk_1", "blk_2", "blk_3")
BLK_GRP = ("blk_0", "blk_1", "blk_2", "blk_3", "grp")


SCALE = 50.0
EPSILON = 1e-06


def from_behind(value, axis, steps):
    count = lax.axis_size(axis)
    pairs = [(source, (source + steps) % count) for source in range(count)]
    return lax.ppermute(value, axis, pairs)


def one_axis_at_a_time(array, axes):
    return functools.reduce(lax.psum, axes, array)


def normalize(raw):
    wide = raw.astype(jnp.float32)
    ratio = lax.rsqrt(jnp.sum(wide * wide, axis=-1, keepdims=True) + EPSILON)
    return ((wide * ratio).astype(jnp.bfloat16), wide, ratio)


def pull_back(grad, wide, ratio):
    inner = jnp.sum(wide * grad, axis=-1, keepdims=True)
    return ratio * grad - ratio * ratio * ratio * inner * wide


def score_block(left, right):
    return SCALE * jnp.einsum("id,jd->ij", left, right, preferred_element_type=jnp.float32)


def transpose_product(weights, left):
    return SCALE * jnp.einsum("ij,id->jd", weights, left, preferred_element_type=jnp.float32)


def on_device(queries, documents, positives):
    norm_q, wide_q, ratio_q = normalize(queries)
    norm_d, wide_d, ratio_d = normalize(documents)
    width = lax.axis_size(BLK)
    far = width // 4
    offsets = [1, -1, far, -far]
    rows = norm_q.shape[0]
    received = [norm_d]
    for off in offsets:
        received.append(from_behind(norm_d, BLK, off))
    scores = [score_block(norm_q, block) for block in received]
    total = scores[0].shape[0] * 0.0 + jnp.zeros((rows,), jnp.float32)
    for block_scores in scores:
        total = total + jnp.sum(jnp.exp(block_scores), axis=-1)
    lse = jnp.log(total)
    columns = jnp.arange(rows, dtype=jnp.int32)
    hot = (columns[None, :] == positives[0][:, None]).astype(jnp.float32)
    spos = jnp.sum(scores[0] * hot, axis=-1)
    part = jnp.sum(lse - spos)
    weights = [(jnp.exp(scores[0] - lse[:, None]) - hot).astype(jnp.bfloat16)]
    for block_scores in scores[1:]:
        weights.append(jnp.exp(block_scores - lse[:, None]).astype(jnp.bfloat16))
    query_dir = jnp.zeros_like(wide_q)
    for weight, block in zip(weights, received):
        query_dir = query_dir + SCALE * jnp.dot(weight, block, preferred_element_type=jnp.float32)
    doc_dir = transpose_product(weights[0], norm_q)
    for off, weight in zip(offsets, weights[1:]):
        partial_grad = transpose_product(weight, norm_q)
        doc_dir = doc_dir + from_behind(partial_grad.astype(jnp.bfloat16), BLK, -off).astype(
            partial_grad.dtype
        )
    query_grad = pull_back(query_dir, wide_q, ratio_q)
    doc_grad = pull_back(doc_dir, wide_d, ratio_d)
    summed = one_axis_at_a_time(part, BLK_GRP)
    loss = summed / (rows * width * lax.axis_size("grp"))
    return (query_grad, doc_grad, loss)


def solution(mesh):
    finer = Mesh(
        mesh.devices.reshape(2, 4, 4, 2, mesh.shape["grp"]),
        ("blk_0", "blk_1", "blk_2", "blk_3", "grp"),
    )
    placed = (P(BLK_GRP, None), P(BLK_GRP, None), P(BLK_GRP, None))
    return jax.shard_map(
        on_device,
        mesh=finer,
        in_specs=placed,
        out_specs=(P(BLK_GRP, None), P(BLK_GRP, None), P()),
        check_vma=False,
    )
```

profile of v0, /device:TPU:10, one launch (start us, length us, event | category | flops | bytes accessed | tf_op | source)
XLA Modules:
  0.0 309.4 jit_solution(10257183670272865154)
XLA Ops:
  0.6 2.2 fusion.10
  2.9 2.2 fusion.11
  5.1 3.6 %collective-permute-start.3 = (bf16[256,4096]{1,0:T(8,128)(2,1)S(1)}, bf16[256,4096]{1,0:T(8,128)(2,1)S(1)}, u32[]{:S(2)}, u32[]{:S(2)}) collective-permute-start(bf16[256,4096]{1,0:T(8,128)(2,1)S(1)} %fusion.11), channel_id=1, source_target_pairs={{0,192},{4,196},{8,200},{12,204},{16,208},{20,212},{24,216},{28,22... | collective-permute-start | bytes 6291464 | tf_op jit(solution)/shard_map/ppermute | solution.py:20
  10.6 88.4 %collective-permute-done.3 = bf16[256,4096]{1,0:T(8,128)(2,1)S(1)} collective-permute-done((bf16[256,4096]{1,0:T(8,128)(2,1)S(1)}, bf16[256,4096]{1,0:T(8,128)(2,1)S(1)}, u32[]{:S(2)}, u32[]{:S(2)}) %collective-permute-start.3) | collective-permute-done | bytes 2097184 | tf_op jit(solution)/shard_map/ppermute | solution.py:20
  100.7 1.0 exponential_reduce_fusion.2
  103.4 2.8 fusion.16
  106.2 2.2 fusion.5
  108.4 2.1 collective-permute-start.7
  110.6 2.3 fusion.4
  112.8 2.3 collective-permute-start.6
  115.1 47.0 %psum.35 = f32[]{:T(128)} all-reduce(f32[]{:T(128)} %get-tuple-element.5), channel_id=1, replica_groups=mesh['blk_0'=2,'blk_1'=4,'blk_2'=4,'blk_3'=2,'grp'=4] {'blk_0'}, use_global_device_ids=true, to_apply=%region_11.0 | all-reduce | flops 1 | bytes 8 | tf_op jit(solution)/shard_map/psum | solution.py:24
  162.1 2.2 fusion.3
  164.3 41.2 %psum.36 = f32[]{:T(128)} all-reduce(f32[]{:T(128)} %psum.35), channel_id=1, replica_groups=mesh['blk_0'=2,'blk_1'=4,'blk_2'=4,'blk_3'=2,'grp'=4] {'blk_1'}, use_global_device_ids=true, to_apply=%region_12.0 | all-reduce | flops 1 | bytes 8 | tf_op jit(solution)/shard_map/psum | solution.py:24
  205.5 41.1 %psum.37 = f32[]{:T(128)} all-reduce(f32[]{:T(128)} %psum.36), channel_id=1, replica_groups=mesh['blk_0'=2,'blk_1'=4,'blk_2'=4,'blk_3'=2,'grp'=4] {'blk_2'}, use_global_device_ids=true, to_apply=%region_13.0 | all-reduce | flops 1 | bytes 8 | tf_op jit(solution)/shard_map/psum | solution.py:24
  246.6 2.2 fusion.2
  248.9 3.1 psum.38
  251.9 19.4 %collective-permute-start.4 = (bf16[256,4096]{1,0:T(8,128)(2,1)}, bf16[256,4096]{1,0:T(8,128)(2,1)}, u32[]{:S(2)}, u32[]{:S(2)}) collective-permute-start(bf16[256,4096]{1,0:T(8,128)(2,1)} %fusion.2), channel_id=1, source_target_pairs={{0,252},{4,0},{8,4},{12,8},{16,12},{20,16},{24,20},{28,24},{32,28}... | collective-permute-start | bytes 6291464 | tf_op jit(solution)/shard_map/ppermute | solution.py:20
  271.4 15.5 %psum.39 = f32[]{:T(128)} all-reduce(f32[]{:T(128)} %psum.38), channel_id=1, replica_groups=mesh['blk_0'=2,'blk_1'=4,'blk_2'=4,'blk_3'=2,'grp'=4] {'grp'}, use_global_device_ids=true, to_apply=%region_15.0 | all-reduce | flops 1 | bytes 8 | tf_op jit(solution)/shard_map/psum | solution.py:24
  287.6 2.5 fusion.15
  290.9 1.4 copy-done.2
  294.5 1.8 fusion.8
  296.4 3.0 fusion.9
  299.4 5.9 %fusion.12 = (f32[256]{0:T(256)S(1)}, f32[256,4096]{1,0:T(8,128)S(1)}) fusion(bf16[256,4096]{1,0:T(8,128)(2,1)S(1)} %copy-done, bf16[256,4096]{1,0:T(8,128)(2,1)} %collective-permute-done.7, bf16[256,4096]{1,0:T(8,128)(2,1)} %collective-permute-done.6, bf16[256,4096]{1,0:T(8,128)(2,1)} %collective-permute-done.5, ...), kind=kOutput, calls=%fused_computation.27 | convolution fusion | flops 552926976 | bytes 17043456 | tf_op jit(solution)/shard_map/ij,id->jd/dot_general | solution.py:43
  305.3 3.0 fusion.13
  (44 shorter events, 8.4 us)
Async XLA Ops:
  0.6 8.6 %copy-start.1 = (bf16[256,4096]{1,0:T(8,128)(2,1)S(1)}, bf16[256,4096]{1,0:T(8,128)(2,1)}, u32[]{:S(2)}) copy-start(bf16[256,4096]{1,0:T(8,128)(2,1)} %param.3) | copy-start | bytes 6291460
  0.6 9.1 %copy-start.10 = (s32[1,256]{1,0:T(1,128)S(1)}, s32[1,256]{1,0:T(1,128)}, u32[]{:S(2)}) copy-start(s32[1,256]{1,0:T(1,128)} %param.5) | copy-start | bytes 3076
  5.1 93.9 %collective-permute-start.3 = (bf16[256,4096]{1,0:T(8,128)(2,1)S(1)}, bf16[256,4096]{1,0:T(8,128)(2,1)S(1)}, u32[]{:S(2)}, u32[]{:S(2)}) collective-permute-start(bf16[256,4096]{1,0:T(8,128)(2,1)S(1)} %fusion.11), channel_id=1, source_target_pairs={{0,192},{4,196},{8,200},{12,204},{16,208},{20,212},{24,216},{28,22... | collective-permute-start | bytes 6291464 | tf_op jit(solution)/shard_map/ppermute | solution.py:20
  8.6 91.2 %collective-permute-start.2 = (bf16[256,4096]{1,0:T(8,128)(2,1)S(1)}, bf16[256,4096]{1,0:T(8,128)(2,1)S(1)}, u32[]{:S(2)}, u32[]{:S(2)}) collective-permute-start(bf16[256,4096]{1,0:T(8,128)(2,1)S(1)} %fusion.11), channel_id=1, source_target_pairs={{0,64},{4,68},{8,72},{12,76},{16,80},{20,84},{24,88},{28,92},{32,9... | collective-permute-start | bytes 6291464 | tf_op jit(solution)/shard_map/ppermute | solution.py:20
  8.7 92.0 %collective-permute-start.1 = (bf16[256,4096]{1,0:T(8,128)(2,1)S(1)}, bf16[256,4096]{1,0:T(8,128)(2,1)S(1)}, u32[]{:S(2)}, u32[]{:S(2)}) collective-permute-start(bf16[256,4096]{1,0:T(8,128)(2,1)S(1)} %fusion.11), channel_id=1, source_target_pairs={{0,252},{4,0},{8,4},{12,8},{16,12},{20,16},{24,20},{28,24},{32,28}... | collective-permute-start | bytes 6291464 | tf_op jit(solution)/shard_map/ppermute | solution.py:20
  8.7 93.1 %collective-permute-start = (bf16[256,4096]{1,0:T(8,128)(2,1)S(1)}, bf16[256,4096]{1,0:T(8,128)(2,1)S(1)}, u32[]{:S(2)}, u32[]{:S(2)}) collective-permute-start(bf16[256,4096]{1,0:T(8,128)(2,1)S(1)} %fusion.11), channel_id=1, source_target_pairs={{0,4},{4,8},{8,12},{12,16},{16,20},{20,24},{24,28},{28,32},{32,36}... | collective-permute-start | bytes 6291464 | tf_op jit(solution)/shard_map/ppermute | solution.py:20
  99.0 1.7 copy-start.3
  99.8 1.9 copy-start.4
  100.7 2.1 copy-start.8
  101.8 4.4 %copy-start.6 = (bf16[256,4096]{1,0:T(8,128)(2,1)}, bf16[256,4096]{1,0:T(8,128)(2,1)S(1)}, u32[]{:S(2)}) copy-start(bf16[256,4096]{1,0:T(8,128)(2,1)S(1)} %collective-permute-done) | copy-start | bytes 6291460
  108.4 191.0 %collective-permute-start.7 = (bf16[256,4096]{1,0:T(8,128)(2,1)}, bf16[256,4096]{1,0:T(8,128)(2,1)}, u32[]{:S(2)}, u32[]{:S(2)}) collective-permute-start(bf16[256,4096]{1,0:T(8,128)(2,1)} %fusion.5), channel_id=1, source_target_pairs={{0,64},{4,68},{8,72},{12,76},{16,80},{20,84},{24,88},{28,92},{32,9... | collective-permute-start | bytes 6291464 | tf_op jit(solution)/shard_map/ppermute | solution.py:20
  112.8 186.6 %collective-permute-start.6 = (bf16[256,4096]{1,0:T(8,128)(2,1)}, bf16[256,4096]{1,0:T(8,128)(2,1)}, u32[]{:S(2)}, u32[]{:S(2)}) collective-permute-start(bf16[256,4096]{1,0:T(8,128)(2,1)} %fusion.4), channel_id=1, source_target_pairs={{0,192},{4,196},{8,200},{12,204},{16,208},{20,212},{24,216},{28,22... | collective-permute-start | bytes 6291464 | tf_op jit(solution)/shard_map/ppermute | solution.py:20
  205.5 93.9 %collective-permute-start.5 = (bf16[256,4096]{1,0:T(8,128)(2,1)}, bf16[256,4096]{1,0:T(8,128)(2,1)}, u32[]{:S(2)}, u32[]{:S(2)}) collective-permute-start(bf16[256,4096]{1,0:T(8,128)(2,1)} %fusion.3), channel_id=1, source_target_pairs={{0,4},{4,8},{8,12},{12,16},{16,20},{20,24},{24,28},{28,32},{32,36}... | collective-permute-start | bytes 6291464 | tf_op jit(solution)/shard_map/ppermute | solution.py:20
  251.9 47.5 %collective-permute-start.4 = (bf16[256,4096]{1,0:T(8,128)(2,1)}, bf16[256,4096]{1,0:T(8,128)(2,1)}, u32[]{:S(2)}, u32[]{:S(2)}) collective-permute-start(bf16[256,4096]{1,0:T(8,128)(2,1)} %fusion.2), channel_id=1, source_target_pairs={{0,252},{4,0},{8,4},{12,8},{16,12},{20,16},{24,20},{28,24},{32,28}... | collective-permute-start | bytes 6291464 | tf_op jit(solution)/shard_map/ppermute | solution.py:20
  287.6 2.5 copy-start.5
  290.1 2.2 copy-start.2
  290.1 2.9 copy-start.7
  293.0 1.6 copy-start.9
  296.4 3.1 copy-start
where the time goes:
time: 310 us; the launch traced here: 309 us
  blocking collectives  148 us (48%)
  waiting for transfers between devices  88.4 us (29%)
  starting transfers between devices  28 us (9%)
  matrix products  27.9 us (9%)
  other arithmetic  11.6 us (4%)
    psum x5, blocking collectives, one_axis_at_a_time(): return functools.reduce(lax.psum, axes, array)  148 us
    ppermute x8, waiting for transfers between devices, from_behind(): return lax.ppermute(value, axis, pairs)  88.4 us
    ppermute x8, starting transfers between devices, from_behind(): return lax.ppermute(value, axis, pairs)  28 us
    dot_general x5, matrix products, transpose_product(): jnp.einsum('ij,id->jd', weights, left, preferred_element_type=jnp.float32)  14.8 us
    dot_general x5, matrix products, on_device(): jnp.dot(weight, block, preferred_element_type=jnp.float32)  8.55 us
  transfers between devices with their start and end apart: 8, of which 1 were waited for; matrix products, arithmetic and copies ran while one was open for 6% of the time, Pallas kernels for 0%

commit v1 on v0

v1 whole, which is shorter than its diff:
```python
import itertools

import jax
import jax.numpy as jnp
from jax import lax
from jax.experimental import pallas as pl
from jax.experimental.pallas import tpu as pltpu
from jax.sharding import Mesh
from jax.sharding import PartitionSpec as P

BLK = ("blk_0", "blk_1", "blk_2", "blk_3")
GRP = "grp"
BLK_GRP = BLK + (GRP,)
NZ, NX, NY, NC = 2, 4, 4, 2

SCALE = 50.0
EPSILON = 1e-06
DOC_CHUNKS = (128, 128)
QUERY_CHUNKS = (128, 128)
STRIPE = 1024
STEP = 64
MIB = 1024 * 1024


def index(z, x, y, c):
    return ((z % NZ * NX + x % NX) * NY + y % NY) * NC + c % NC


def table(target):
    pairs = []
    for at in itertools.product(range(NZ), range(NX), range(NY), range(NC)):
        to = target(*at)
        if to is not None:
            pairs.append((index(*at), index(*to)))
    return pairs


def is_edge(y, c):
    return (y == NY - 1 and c == 1) or (y == 0 and c == 0)


def off_chip(z, x, y, c):
    step = 1 if c == 1 else -1
    me = index(z, x, y, c)
    other = (me + step) % (NZ * NX * NY * NC)
    return (other // (NX * NY * NC), other // (NY * NC) % NX, other // NC % NY, other % NC)


def to_holder(z, x, y, c):
    if not is_edge(y, c):
        return None
    if c == 1:
        return (z + (x == NX - 1), x, 0, 0)
    return (z + (x == 0), x, NY - 1, 1)


def from_holder(z, x, y, c):
    if not is_edge(y, c):
        return off_chip(z, x, y, c)
    return (z, x + 1, y, c) if c == 0 else (z, x - 1, y, c)


ON_CHIP = table(lambda z, x, y, c: (z, x, y, 1 - c))
OFF_CHIP = table(off_chip)
TO_HOLDER = table(to_holder)
FROM_HOLDER = table(from_holder)
ACROSS_X = table(lambda z, x, y, c: (z, x + 2, y, c))
ACROSS_Z = table(lambda z, x, y, c: (z + 1, x, y, c))
ACROSS_XZ = table(lambda z, x, y, c: (z + 1, x + 2, y, c))


def permute(value, pairs):
    return lax.ppermute(value, BLK, pairs)


def after(value, *others):
    others = [o for o in others if o is not None]
    if not others:
        return value
    return lax.optimization_barrier((value, *others))[0]


ANY = pl.BlockSpec(memory_space=pl.ANY)
VMEM = pl.BlockSpec(memory_space=pltpu.VMEM)


def call(kernel, inputs, outputs, scratch, *, any_in, any_out):
    return pl.pallas_call(
        kernel,
        in_specs=[ANY if a else VMEM for a in any_in],
        out_specs=[ANY if a else VMEM for a in any_out],
        out_shape=outputs,
        scratch_shapes=scratch,
        cost_estimate=pl.CostEstimate(flops=1024, bytes_accessed=1024, transcendentals=0),
        compiler_params=pltpu.CompilerParams(vmem_limit_bytes=60 * MIB),
    )(*inputs)


def shape(rows, columns, kind):
    return jax.ShapeDtypeStruct((rows, columns), kind)


def start(source, target, sem):
    copy = pltpu.make_async_copy(source, target, sem)
    copy.start()
    return copy


def normalize(raw, chunks):
    rows, width = raw.shape
    spans = [(0, rows)]
    for sizes in chunks:
        spans += [(sum(sizes[:k]), size) for k, size in enumerate(sizes)]
    n, steps = len(spans), rows // STEP

    def kernel(raw, *refs):
        outs, ratio = refs[:n], refs[n]
        before, result, sems, out_sems = refs[n + 1 :]
        loads = [
            start(raw.at[pl.ds(k * STEP, STEP)], before.at[pl.ds(k * STEP, STEP)], sems.at[k])
            for k in range(steps)
        ]
        stores = []
        for k in range(steps):
            own = pl.ds(k * STEP, STEP)
            loads[k].wait()
            wide = before[own].astype(jnp.float32)
            scale = lax.rsqrt(jnp.sum(wide * wide, axis=-1, keepdims=True) + EPSILON)
            ratio[own] = scale
            result[own] = (wide * scale).astype(jnp.bfloat16)
            for j, (at, size) in enumerate(spans):
                if k * STEP < at + size <= (k + 1) * STEP:
                    stores.append(start(result.at[pl.ds(at, size)], outs[j], out_sems.at[j]))
        for copy in stores:
            copy.wait()

    kind = jnp.bfloat16
    return call(
        kernel,
        [raw],
        [shape(size, width, kind) for _, size in spans] + [shape(rows, 1, jnp.float32)],
        [
            pltpu.VMEM((rows, width), kind),
            pltpu.VMEM((rows, width), kind),
            pltpu.SemaphoreType.DMA((steps,)),
            pltpu.SemaphoreType.DMA((n,)),
        ],
        any_in=[True],
        any_out=[True] * n + [False],
    )


def places(blocks):
    at, found = 0, []
    for block in blocks:
        found.append((at, block.shape[0]))
        at += block.shape[0]
    return found, at


def diagonal(size):
    return lax.broadcasted_iota(jnp.int32, (size, size), 0) == lax.broadcasted_iota(
        jnp.int32, (size, size), 1
    )


def column_of(row):
    return jnp.sum(jnp.where(diagonal(row.shape[1]), row, 0), axis=1, keepdims=True)


def row_of(column):
    return jnp.sum(jnp.where(diagonal(column.shape[0]), column, 0), axis=0, keepdims=True)


def scores_of(own, block):
    return SCALE * lax.dot_general(
        own, block, (((1,), (1,)), ((), ())), preferred_element_type=jnp.float32
    )


def groups_of(found, rows):
    runs = []
    for k, (at, size) in enumerate(found):
        if runs and at + size - runs[-1][1] <= rows:
            runs[-1] = (runs[-1][0] + [k], runs[-1][1], at + size - runs[-1][1])
        else:
            runs.append(([k], at, size))
    return runs


def query_side(norm, positive, blocks):
    rows, width = norm.shape
    found, depth = places(blocks)
    n = len(blocks)

    def kernel(norm, positive, *refs):
        blocks, (lse_out, part_out, weights_out, inner_out) = refs[:n], refs[n : n + 4]
        own, buffer, scores, sems = refs[n + 4 :]
        first = start(norm, own, sems.at[n])
        loads = [
            start(blocks[k], buffer.at[pl.ds(at, size)], sems.at[k])
            for k, (at, size) in enumerate(found)
        ]
        first.wait()
        total = jnp.zeros((rows, 1), jnp.float32)
        for members, at, size in groups_of(found, rows):
            for k in members:
                loads[k].wait()
            here = scores_of(own[...], buffer[at : at + size])
            scores[:, at : at + size] = here
            total += jnp.sum(jnp.exp(here), axis=-1, keepdims=True)
        lse = jnp.log(total)
        lse_out[...] = row_of(lse)
        target = column_of(positive[...])
        spos = jnp.zeros((rows, 1), jnp.float32)
        inner = jnp.zeros((rows, 1), jnp.float32)
        for at in range(0, depth, rows):
            here = scores[:, at : at + rows]
            weights = jnp.exp(here - lse)
            if at < 2 * rows:
                hot = lax.broadcasted_iota(jnp.int32, (rows, rows), 1) + at == target
                hot = hot.astype(jnp.float32)
                spos += jnp.sum(here * hot, axis=-1, keepdims=True)
                weights = weights - hot
            weights = weights.astype(jnp.bfloat16)
            weights_out[:, at : at + rows] = weights
            inner += jnp.sum(weights.astype(jnp.float32) * here, axis=-1, keepdims=True)
        inner_out[...] = inner
        part = jnp.sum(lse - spos, axis=0, keepdims=True)
        part_out[...] = jnp.broadcast_to(part, part_out.shape)

    return call(
        kernel,
        [norm, positive, *blocks],
        [
            shape(1, rows, jnp.float32),
            shape(8, 128, jnp.float32),
            shape(rows, depth, jnp.bfloat16),
            shape(rows, 1, jnp.float32),
        ],
        [
            pltpu.VMEM((rows, width), jnp.bfloat16),
            pltpu.VMEM((depth, width), jnp.bfloat16),
            pltpu.VMEM((rows, depth), jnp.float32),
            pltpu.SemaphoreType.DMA((n + 1,)),
        ],
        any_in=[True, False] + [True] * n,
        any_out=[False] * 4,
    )


def query_gradient(weights, inner, ratio, raw, blocks):
    rows, width = raw.shape
    found, depth = places(blocks)
    n, stripes = len(blocks), width // STRIPE

    def kernel(weights, inner, ratio, raw, *refs):
        blocks, out, done = refs[:n], refs[n], refs[n + 1]
        buffer, wide, result, sems, out_sems = refs[n + 2 :]
        done[...] = jnp.zeros_like(done)
        loads = []
        for s in range(stripes):
            at_s = pl.ds(s * STRIPE, STRIPE)
            loads.append(
                [
                    start(blocks[k].at[:, at_s], buffer.at[pl.ds(at, size), at_s], sems.at[s, k])
                    for k, (at, size) in enumerate(found)
                ]
                + [start(raw.at[:, at_s], wide.at[:, at_s], sems.at[s, n])]
            )
        gain = SCALE * ratio[...]
        coef = ratio[...] * ratio[...] * inner[...]
        stores = []
        for s in range(stripes):
            here = slice(s * STRIPE, (s + 1) * STRIPE)
            for copy in loads[s]:
                copy.wait()
            direction = jnp.dot(weights[...], buffer[:, here], preferred_element_type=jnp.float32)
            result[:, here] = gain * direction - coef * wide[:, here].astype(jnp.float32)
            at_s = pl.ds(s * STRIPE, STRIPE)
            stores.append(start(result.at[:, at_s], out.at[:, at_s], out_sems.at[s]))
        for copy in stores:
            copy.wait()

    return call(
        kernel,
        [weights, inner, ratio, raw, *blocks],
        [shape(rows, width, jnp.float32), shape(8, 128, jnp.float32)],
        [
            pltpu.VMEM((depth, width), jnp.bfloat16),
            pltpu.VMEM((rows, width), jnp.bfloat16),
            pltpu.VMEM((rows, width), jnp.float32),
            pltpu.SemaphoreType.DMA((stripes, n + 1)),
            pltpu.SemaphoreType.DMA((stripes,)),
        ],
        any_in=[False] * 3 + [True] * (n + 1),
        any_out=[True, False],
    )


def document_side(norm, positive, lses, blocks, last=None):
    rows, width = norm.shape
    found, depth = places(blocks)
    n, stripes = len(blocks), width // STRIPE
    given = [] if positive is None else [positive]
    small = given + [lses] + ([] if last is None else [last[0], last[3]])
    large = [norm, *blocks] + ([] if last is None else [last[1], last[2]])
    m = len(small)

    def kernel(*refs):
        smalls, (norm, *blocks) = refs[:m], refs[m : m + 1 + n]
        rest = refs[m + 1 + n :]
        lses = smalls[len(given)]
        if last is not None:
            ratio, before_inner = smalls[-2:]
            raw, before = rest[:2]
            rest = rest[2:]
        out, rest = rest[0], rest[1:]
        if last is None:
            inner_out, rest = rest[0], rest[1:]
        own, buffer, result, wide, sems, more_sems, out_sems = rest
        first = start(norm, own, sems.at[n])
        loads = [
            start(blocks[k], buffer.at[pl.ds(at, size)], sems.at[k])
            for k, (at, size) in enumerate(found)
        ]
        more = []
        if last is not None:
            for s in range(stripes):
                at_s = pl.ds(s * STRIPE, STRIPE)
                more.append(
                    [
                        start(raw.at[:, at_s], wide.at[:, at_s], more_sems.at[s, 0]),
                        start(before.at[:, at_s], result.at[:, at_s], more_sems.at[s, 1]),
                    ]
                )
        first.wait()
        inner = jnp.zeros((rows, 1), jnp.float32) if last is None else before_inner[...]
        weights = []
        for members, at, size in groups_of(found, rows):
            for k in members:
                loads[k].wait()
            here = scores_of(own[...], buffer[at : at + size])
            weight = jnp.exp(here - lses[:, at : at + size])
            if at < 2 * rows and given:
                hot = lax.broadcasted_iota(jnp.int32, (rows, size), 0)
                hot = hot == smalls[0][:, at : at + size]
                weight = weight - hot.astype(jnp.float32)
            weight = weight.astype(jnp.bfloat16)
            inner += jnp.sum(weight.astype(jnp.float32) * here, axis=-1, keepdims=True)
            weights.append((weight, at, size))
        if last is None:
            inner_out[...] = inner
        else:
            gain = SCALE * ratio[...]
            coef = ratio[...] * ratio[...] * inner
        stores = []
        for s in range(stripes):
            here = slice(s * STRIPE, (s + 1) * STRIPE)
            direction = None
            for weight, at, size in weights:
                term = jnp.dot(
                    weight, buffer[at : at + size, here], preferred_element_type=jnp.float32
                )
                direction = term if direction is None else direction + term
            if last is not None:
                for copy in more[s]:
                    copy.wait()
                direction = gain * (direction + result[:, here])
                direction = direction - coef * wide[:, here].astype(jnp.float32)
            result[:, here] = direction
            at_s = pl.ds(s * STRIPE, STRIPE)
            stores.append(start(result.at[:, at_s], out.at[:, at_s], out_sems.at[s]))
        for copy in stores:
            copy.wait()

    outputs = [shape(rows, width, jnp.float32)]
    if last is None:
        outputs.append(shape(rows, 1, jnp.float32))
    return call(
        kernel,
        small + large,
        outputs,
        [
            pltpu.VMEM((rows, width), jnp.bfloat16),
            pltpu.VMEM((depth, width), jnp.bfloat16),
            pltpu.VMEM((rows, width), jnp.float32),
            pltpu.VMEM((rows, width), jnp.bfloat16),
            pltpu.SemaphoreType.DMA((n + 1,)),
            pltpu.SemaphoreType.DMA((stripes, 2)),
            pltpu.SemaphoreType.DMA((stripes,)),
        ],
        any_in=[False] * m + [True] * len(large),
        any_out=[True] + [False] * (last is None),
    )


def total_over(value, axes):
    count = 1
    for axis in axes:
        count *= lax.axis_size(axis)
    parts = [
        lax.ppermute(value, axes, [(s, (s + step) % count) for s in range(count)])
        for step in range(1, count)
    ]
    for part in parts:
        value = value + part
    return value


def on_device(queries, documents, positives):
    rows = queries.shape[0]
    y = lax.axis_index("blk_2")
    c = lax.axis_index("blk_3")
    edge = ((y == NY - 1) & (c == 1)) | ((y == 0) & (c == 0))
    n, tail = len(DOC_CHUNKS), QUERY_CHUNKS[-1]
    halves = (rows // 2, rows // 2)

    norm_d, *pieces_d, ratio_d = normalize(documents, [DOC_CHUNKS, halves])
    norm_q, *pieces_q, ratio_q = normalize(queries, [QUERY_CHUNKS])
    halves_d, pieces_d = pieces_d[-2:], pieces_d[:-2]

    pair_d = lax.all_gather(norm_d, "blk_3", tiled=True)
    pair_q = lax.all_gather(norm_q, "blk_3", tiled=True)

    far, farther = [], []
    for k, part in enumerate(pieces_d + pieces_q):
        gates = [] if k < 2 else far[:2] + farther[:1]
        far.append(permute(after(part, *gates), ACROSS_X))
        farther.append(permute(far[k], ACROSS_Z))

    held_d = permute(halves_d[1], TO_HOLDER)
    near_d = [
        permute(after(halves_d[0], far[1]), OFF_CHIP),
        permute(after(jnp.where(edge, held_d, halves_d[1]), far[1]), FROM_HOLDER),
    ]
    held_q = permute(after(norm_q, held_d), TO_HOLDER)
    near_q = permute(after(jnp.where(edge, held_q, norm_q), far[-1]), FROM_HOLDER)

    docs = [pair_d, *near_d] + far[:n] + farther[:n]
    target = jnp.where(c == 0, positives, positives + rows)
    lse, part, weights, inner = query_side(norm_q, target, docs)

    message = after(lse, farther[n])
    other = permute(message, ON_CHIP)
    near_lse = permute(message, OFF_CHIP)
    far_lse = permute(message, ACROSS_X)
    farther_lse = permute(message, ACROSS_XZ)
    none = jnp.full_like(positives, -1)
    first = jnp.where(c == 0, lse, other)
    second = jnp.where(c == 0, other, lse)
    marks = jnp.where(c == 0, jnp.concatenate([positives, none], 1), jnp.concatenate([none, positives], 1))

    query_grad, done = query_gradient(weights, inner, ratio_q, queries, docs)
    early = jnp.concatenate([first, second, far_lse, farther_lse[:, :-tail]], axis=1)
    early = after(early, query_grad)
    direction, inner = document_side(norm_d, marks, early, [pair_q] + far[n:] + farther[n:-1])
    late = jnp.concatenate([near_lse, farther_lse[:, -tail:]], axis=1)
    doc_grad = document_side(
        norm_d, None, late, [near_q, farther[-1]], last=(ratio_d, documents, direction, inner)
    )[0]

    loss = part
    groups = (("blk_0", "blk_3"), ("blk_2",), ("grp",), ("blk_1",))
    for axes, gate in zip(groups, (farther[n], None, farther[-1], None)):
        loss = total_over(after(loss, gate), axes)
    loss = loss[0, 0] / (rows * NZ * NX * NY * NC * lax.axis_size(GRP))
    return query_grad, doc_grad, loss


def solution(mesh):
    finer = Mesh(mesh.devices.reshape(NZ, NX, NY, NC, mesh.shape["grp"]), BLK_GRP)
    rows = P(BLK_GRP, None)
    return jax.shard_map(
        on_device,
        mesh=finer,
        in_specs=(rows, rows, rows),
        out_specs=(rows, rows, P()),
        check_vma=False,
    )
```

time: 310 us -> 231 us (0.75); the launches traced: 309 us -> 227 us
  blocking collectives: 148 us -> 0 us
  Pallas kernels: 0 us -> 51.9 us
  starting transfers between devices: 28 us -> 74.1 us
  matrix products: 27.9 us -> 0 us
  between operations: 2.61 us -> 16.1 us
  waiting for transfers between devices: 88.4 us -> 77.7 us
  other arithmetic: 11.6 us -> 5.35 us
    psum x5 -> x0, blocking collectives: 148 us -> none  [one_axis_at_a_time(): return functools.reduce(lax.psum, axes, array)]
    pallas_call x0 -> x6, Pallas kernels: none -> 51.9 us  [call(): pl.pallas_call(kernel, in_specs=[ANY if a else VMEM for a in any_in], out...]
    ppermute x8 -> x29, starting transfers between devices: 28 us -> 74.1 us  [the longest x12 49 us: total_over(): lax.ppermute(value, axes, [(s, (s + step) % count) for s in range(count)])]
    dot_general x15 -> x0, matrix products: 27.9 us -> none  [the longest x5 14.8 us: transpose_product(): jnp.einsum('ij,id->jd', weights, left, preferred_element_type=jnp.float32)]
    ppermute x8 -> x29, waiting for transfers between devices: 88.4 us -> 77.6 us  [the longest x17 72.9 us: permute(): return lax.ppermute(value, BLK, pairs)]
    sub x2 -> x0, other arithmetic: 6.02 us -> none  [pull_back(): return ratio * grad - ratio * ratio * ratio * inner * wide]
    select_n x0 -> x5, other arithmetic: none -> 4.16 us  [the longest x1 1.64 us: on_device(): jnp.where(edge, held_q, norm_q)]
    reduce_sum x3 -> x0, other arithmetic: 3.34 us -> none  [the longest x2 2.72 us: normalize(): ratio = lax.rsqrt(jnp.sum(wide * wide, axis=-1, keepdims=True) + EPSILON)]
  transfers between devices with their start and end apart: 8 -> 31, of which waited for: 1 -> 8; matrix products, arithmetic and copies ran while one was open for 6% -> 3% of each run, Pallas kernels for 0% -> 16%
where the time goes in v1:
time: 231 us; the launch traced here: 227 us
  waiting for transfers between devices  77.7 us (34%)
  starting transfers between devices  74.1 us (32%)
  Pallas kernels  51.9 us (22%)
  between operations  16.1 us (7%)
  other arithmetic  5.35 us (2%)
    ppermute x17, waiting for transfers between devices, permute(): return lax.ppermute(value, BLK, pairs)  72.9 us
    pallas_call x6, Pallas kernels, call(): pl.pallas_call(kernel, in_specs=[ANY if a else VMEM for a in any_in], out...  51.9 us
    ppermute x12, starting transfers between devices, total_over(): lax.ppermute(value, axes, [(s, (s + step) % count) for s in range(count)])  49 us
    ppermute x17, starting transfers between devices, permute(): return lax.ppermute(value, BLK, pairs)  25 us
    ppermute x12, waiting for transfers between devices, total_over(): lax.ppermute(value, axes, [(s, (s + step) % count) for s in range(count)])  4.75 us
  transfers between devices with their start and end apart: 31, of which 8 were waited for; matrix products, arithmetic and copies ran while one was open for 3% of the time, Pallas kernels for 16%

profile of v1, /device:TPU:10, one launch (start us, length us, event | category | flops | bytes accessed | tf_op | source)
XLA Modules:
  0.0 227.0 jit_solution(2335714685652631772)
XLA Ops:
  7.2 4.9 %shard_map.59 = (bf16[256,4096]{1,0:T(8,128)(2,1)}, bf16[128,4096]{1,0:T(8,128)(2,1)}, bf16[128,4096]{1,0:T(8,128)(2,1)}, bf16[128,4096]{1,0:T(8,128)(2,1)}, bf1...) custom-call(bf16[256,4096]{1,0:T(8,128)(2,1)} %refs_6_.1), custom_call_target="tpu_custom_call" | custom-call | flops 1024 | bytes 1024 | tf_op jit(solution)/shard_map/pallas_call | solution.py:88
  12.2 2.2 collective-permute-start.4
  16.6 23.4 %collective-permute-done.4.refs_3_ = bf16[128,4096]{1,0:T(8,128)(2,1)S(1)} collective-permute-done((bf16[128,4096]{1,0:T(8,128)(2,1)}, bf16[128,4096]{1,0:T(8,128)(2,1)S(1)}, u32[]{:S(2)}, u32[]{:S(2)}) %collective-permute-start.4) | collective-permute-done | bytes 1048608 | tf_op jit(solution)/shard_map/ppermute | solution.py:73
  40.0 1.9 collective-permute-start.5
  41.9 4.3 %shard_map.58 = (bf16[256,4096]{1,0:T(8,128)(2,1)}, bf16[128,4096]{1,0:T(8,128)(2,1)}, bf16[128,4096]{1,0:T(8,128)(2,1)}, f32[256,1]{1,0:T(8,128)}) custom-call(bf16[256,4096]{1,0:T(8,128)(2,1)} %raw.5), custom_call_target="tpu_custom_call" | custom-call | flops 1024 | bytes 1024 | tf_op jit(solution)/shard_map/pallas_call | solution.py:88
  46.3 2.0 collective-permute-start.14
  48.3 13.1 %collective-permute-done.refs_4_ = bf16[128,4096]{1,0:T(8,128)(2,1)} collective-permute-done((bf16[128,4096]{1,0:T(8,128)(2,1)}, bf16[128,4096]{1,0:T(8,128)(2,1)}, u32[]{:S(2)}, u32[]{:S(2)}) %collective-permute-start) | collective-permute-done | bytes 1048608 | tf_op jit(solution)/shard_map/ppermute | solution.py:73
  63.2 2.1 collective-permute-start.7
  70.2 17.1 %collective-permute-done.7.refs_4_ = bf16[128,4096]{1,0:T(8,128)(2,1)} collective-permute-done((bf16[128,4096]{1,0:T(8,128)(2,1)}, bf16[128,4096]{1,0:T(8,128)(2,1)}, u32[]{:S(2)}, u32[]{:S(2)}) %collective-permute-start.7) | collective-permute-done | bytes 1048608 | tf_op jit(solution)/shard_map/ppermute | solution.py:73
  87.3 2.1 collective-permute-start.13
  93.0 17.5 %collective-permute-done.13.refs_5_ = bf16[128,4096]{1,0:T(8,128)(2,1)} collective-permute-done((bf16[128,4096]{1,0:T(8,128)(2,1)}, bf16[128,4096]{1,0:T(8,128)(2,1)}, u32[]{:S(2)}, u32[]{:S(2)}) %collective-permute-start.13) | collective-permute-done | bytes 1048608 | tf_op jit(solution)/shard_map/ppermute | solution.py:73
  110.8 2.1 collective-permute-start.16
  113.5 10.9 %shard_map.60 = (f32[1,256]{1,0:T(1,128)}, f32[8,128]{1,0:T(8,128)}, bf16[256,1280]{1,0:T(8,128)(2,1)}, f32[256,1]{1,0:T(8,128)}) custom-call(bf16[256,4096]{1,0:T(8,128)(2,1)} %get-tuple-element.51.norm, s32[1,256]{1,0:T(1,128)} %broadcast_select_fusion.5.positive, bf16[512,4096]{1,0:T(8,128)(2,1)} %all-gather.3.cloned.1.call-done.refs_0_, ...), custom_call_target="tpu_custom_call" | custom-call | flops 1024 | bytes 1024 | tf_op jit(solution)/shard_map/pallas_call | solution.py:88
  127.8 9.3 %shard_map.61 = (f32[256,4096]{1,0:T(8,128)}, f32[8,128]{1,0:T(8,128)}) custom-call(bf16[256,1280]{1,0:T(8,128)(2,1)} %get-tuple-element.38.weights, f32[256,1]{1,0:T(8,128)} %get-tuple-element.39.inner, f32[256,1]{1,0:T(8,128)} %get-tuple-element.40.ratio, bf16[256,4096]{1,0:T(8,128)(2,1)} %raw.5, bf16[512,4096]{1,0:T(8,128)(2,1)} %all-gather.3.cloned.1.call-done.refs_0_, ...), custom_call_target="tpu_custom_call" | custom-call | flops 1024 | bytes 1024 | tf_op jit(solution)/shard_map/pallas_call | solution.py:88
  140.2 15.2 %collective-permute-start.22 = (f32[8,128]{1,0:T(8,128)S(1)}, f32[8,128]{1,0:T(8,128)S(1)}, u32[]{:S(2)}, u32[]{:S(2)}) collective-permute-start(f32[8,128]{1,0:T(8,128)S(1)} %add_add_fusion.3), channel_id=1, source_target_pairs={{0,24},{8,0},{16,8},{24,16},{1,25},{9,1},{17,9},{25,17},{2,26},{10... | collective-permute-start | bytes 12296 | tf_op jit(solution)/shard_map/ppermute | solution.py:403
  155.4 15.8 %collective-permute-start.21 = (f32[8,128]{1,0:T(8,128)S(1)}, f32[8,128]{1,0:T(8,128)S(1)}, u32[]{:S(2)}, u32[]{:S(2)}) collective-permute-start(f32[8,128]{1,0:T(8,128)S(1)} %add_add_fusion.3), channel_id=1, source_target_pairs={{0,16},{8,24},{16,0},{24,8},{1,17},{9,25},{17,1},{25,9},{2,18},{10... | collective-permute-start | bytes 12296 | tf_op jit(solution)/shard_map/ppermute | solution.py:403
  171.2 2.5 %collective-permute-start.20 = (f32[8,128]{1,0:T(8,128)S(1)}, f32[8,128]{1,0:T(8,128)S(1)}, u32[]{:S(2)}, u32[]{:S(2)}) collective-permute-start(f32[8,128]{1,0:T(8,128)S(1)} %add_add_fusion.3), channel_id=1, source_target_pairs={{0,8},{8,16},{16,24},{24,0},{1,9},{9,17},{17,25},{25,1},{2,10},{10... | collective-permute-start | bytes 12296 | tf_op jit(solution)/shard_map/ppermute | solution.py:403
  173.8 2.1 collective-permute-start.12
  175.9 6.1 %collective-permute-start.25 = (f32[8,128]{1,0:T(8,128)S(1)}, f32[8,128]{1,0:T(8,128)S(1)}, u32[]{:S(2)}, u32[]{:S(2)}) collective-permute-start(f32[8,128]{1,0:T(8,128)S(1)} %add_add_fusion.2), channel_id=1, source_target_pairs={{0,3},{1,0},{2,1},{3,2},{4,7},{5,4},{6,5},{7,6},{8,11},{9,8},{10,9... | collective-permute-start | bytes 12296 | tf_op jit(solution)/shard_map/ppermute | solution.py:403
  182.9 2.8 %collective-permute-start.23 = (f32[8,128]{1,0:T(8,128)S(1)}, f32[8,128]{1,0:T(8,128)S(1)}, u32[]{:S(2)}, u32[]{:S(2)}) collective-permute-start(f32[8,128]{1,0:T(8,128)S(1)} %add_add_fusion.2), channel_id=1, source_target_pairs={{0,1},{1,2},{2,3},{3,0},{4,5},{5,6},{6,7},{7,4},{8,9},{9,10},{10,1... | collective-permute-start | bytes 12296 | tf_op jit(solution)/shard_map/ppermute | solution.py:403
  186.4 3.1 %collective-permute-done.24 = f32[8,128]{1,0:T(8,128)S(1)} collective-permute-done((f32[8,128]{1,0:T(8,128)S(1)}, f32[8,128]{1,0:T(8,128)S(1)}, u32[]{:S(2)}, u32[]{:S(2)}) %collective-permute-start.24) | collective-permute-done | bytes 4128 | tf_op jit(solution)/shard_map/ppermute | solution.py:403
  191.0 2.3 %collective-permute-start.26 = (f32[8,128]{1,0:T(8,128)S(1)}, f32[8,128]{1,0:T(8,128)S(1)}, u32[]{:S(2)}, u32[]{:S(2)}) collective-permute-start(f32[8,128]{1,0:T(8,128)S(1)} %add_add_fusion.1), channel_id=1, source_target_pairs={{0,32},{32,64},{64,96},{96,0},{1,33},{33,65},{65,97},{97,1},{2,34}... | collective-permute-start | bytes 12296 | tf_op jit(solution)/shard_map/ppermute | solution.py:403
  193.9 11.6 %shard_map.62 = (f32[256,4096]{1,0:T(8,128)}, f32[256,1]{1,0:T(8,128)}) custom-call(s32[1,512]{1,0:T(1,128)} %broadcast_select_fusion.2.refs_0_, f32[1,896]{1,0:T(1,128)} %pad_maximum_fusion.refs_1_, bf16[256,4096]{1,0:T(8,128)(2,1)} %get-tuple-element.31.refs_2_.refs_3_, bf16[512,4096]{1,0:T(8,128)(2,1)} %all-gather.5.cloned.1.call-done.refs_3_, ...), custom_call_target="tpu_custom_call" | custom-call | flops 1024 | bytes 1024 | tf_op jit(solution)/shard_map/pallas_call | solution.py:88
  208.1 10.9 %shard_map.63 = f32[256,4096]{1,0:T(8,128)} custom-call(f32[1,384]{1,0:T(1,128)} %pad_maximum_fusion.1.refs_0_, f32[256,1]{1,0:T(8,128)} %get-tuple-element.46.refs_1_, f32[256,1]{1,0:T(8,128)} %get-tuple-element.50.refs_2_, bf16[256,4096]{1,0:T(8,128)(2,1)} %get-tuple-element.31.refs_2_.refs_3_, bf16[256,4096]{1,0:T(8,128)(2,1)} %copy-done.3, ...), custom_call_target="tpu_custom_call" | custom-call | flops 1024 | bytes 1024 | tf_op jit(solution)/shard_map/pallas_call | solution.py:88
  (77 shorter events, 25.6 us)
Async XLA Ops:
  7.2 106.3 %all-gather.3.cloned.1.call-start = ((), (), s32[]{:S(2)}) async-start(), calls=%async_computation | async-start | bytes 6291456 | tf_op jit(solution)/shard_map/all_gather | solution.py:423
  12.1 181.8 %all-gather.5.cloned.1.call-start = ((), (), s32[]{:S(2)}) async-start(), calls=%async_computation.1 | async-start | bytes 6291456 | tf_op jit(solution)/shard_map/all_gather | solution.py:424
  12.2 27.8 %collective-permute-start.4 = (bf16[128,4096]{1,0:T(8,128)(2,1)}, bf16[128,4096]{1,0:T(8,128)(2,1)S(1)}, u32[]{:S(2)}, u32[]{:S(2)}) collective-permute-start(bf16[128,4096]{1,0:T(8,128)(2,1)} %get-tuple-element.37), channel_id=1, source_target_pairs={{0,64},{4,68},{8,72},{12,76},{16,80},{20,84},{24,88},{28,92},{32,9... | collective-permute-start | bytes 3145736 | tf_op jit(solution)/shard_map/ppermute | solution.py:73
  14.4 31.9 %collective-permute-start.2 = (bf16[128,4096]{1,0:T(8,128)(2,1)S(1)}, bf16[128,4096]{1,0:T(8,128)(2,1)S(1)}, u32[]{:S(2)}, u32[]{:S(2)}) collective-permute-start(bf16[128,4096]{1,0:T(8,128)(2,1)S(1)} %copy-done.4), channel_id=1, source_target_pairs={{0,156},{28,0},{32,60},{60,32},{64,92},{92,64},{96,124},{124,224},... | collective-permute-start | bytes 3145736 | tf_op jit(solution)/shard_map/ppermute | solution.py:73
  15.1 46.3 %collective-permute-start = (bf16[128,4096]{1,0:T(8,128)(2,1)}, bf16[128,4096]{1,0:T(8,128)(2,1)}, u32[]{:S(2)}, u32[]{:S(2)}) collective-permute-start(bf16[128,4096]{1,0:T(8,128)(2,1)} %get-tuple-element.33), channel_id=1, source_target_pairs={{0,64},{4,68},{8,72},{12,76},{16,80},{20,84},{24,88},{28,92},{32,9... | collective-permute-start | bytes 3145736 | tf_op jit(solution)/shard_map/ppermute | solution.py:73
  40.0 23.2 %collective-permute-start.5 = (bf16[128,4096]{1,0:T(8,128)(2,1)S(1)}, bf16[128,4096]{1,0:T(8,128)(2,1)}, u32[]{:S(2)}, u32[]{:S(2)}) collective-permute-start(bf16[128,4096]{1,0:T(8,128)(2,1)S(1)} %collective-permute-done.4.refs_3_), channel_id=1, source_target_pairs={{0,128},{4,132},{8,136},{12,140},{16,144},{20,148},{24,152},{28,15... | collective-permute-start | bytes 3145736 | tf_op jit(solution)/shard_map/ppermute | solution.py:73
  46.3 43.1 %collective-permute-start.14 = (bf16[256,4096]{1,0:T(8,128)(2,1)}, bf16[256,4096]{1,0:T(8,128)(2,1)}, u32[]{:S(2)}, u32[]{:S(2)}) collective-permute-start(bf16[256,4096]{1,0:T(8,128)(2,1)} %get-tuple-element.51.norm), channel_id=1, source_target_pairs={{0,156},{28,0},{32,60},{60,32},{64,92},{92,64},{96,124},{124,224},... | collective-permute-start | bytes 6291464 | tf_op jit(solution)/shard_map/ppermute | solution.py:73
  63.2 24.1 %collective-permute-start.7 = (bf16[128,4096]{1,0:T(8,128)(2,1)}, bf16[128,4096]{1,0:T(8,128)(2,1)}, u32[]{:S(2)}, u32[]{:S(2)}) collective-permute-start(bf16[128,4096]{1,0:T(8,128)(2,1)} %get-tuple-element.44), channel_id=1, source_target_pairs={{0,64},{4,68},{8,72},{12,76},{16,80},{20,84},{24,88},{28,92},{32,9... | collective-permute-start | bytes 3145736 | tf_op jit(solution)/shard_map/ppermute | solution.py:73
  65.3 45.5 %collective-permute-start.1 = (bf16[128,4096]{1,0:T(8,128)(2,1)}, bf16[128,4096]{1,0:T(8,128)(2,1)S(1)}, u32[]{:S(2)}, u32[]{:S(2)}) collective-permute-start(bf16[128,4096]{1,0:T(8,128)(2,1)} %get-tuple-element.34), channel_id=1, source_target_pairs={{0,252},{4,8},{8,4},{12,16},{16,12},{20,24},{24,20},{28,32},{32,28... | collective-permute-start | bytes 3145736 | tf_op jit(solution)/shard_map/ppermute | solution.py:73
  66.7 46.7 %collective-permute-start.3 = (bf16[128,4096]{1,0:T(8,128)(2,1)S(1)}, bf16[128,4096]{1,0:T(8,128)(2,1)}, u32[]{:S(2)}, u32[]{:S(2)}) collective-permute-start(bf16[128,4096]{1,0:T(8,128)(2,1)S(1)} %broadcast_select_fusion.1), channel_id=1, source_target_pairs={{0,32},{4,8},{8,4},{12,16},{16,12},{20,24},{24,20},{28,124},{32,64... | collective-permute-start | bytes 3145736 | tf_op jit(solution)/shard_map/ppermute | solution.py:73
  68.5 45.0 %collective-permute-start.6 = (bf16[128,4096]{1,0:T(8,128)(2,1)}, bf16[128,4096]{1,0:T(8,128)(2,1)}, u32[]{:S(2)}, u32[]{:S(2)}) collective-permute-start(bf16[128,4096]{1,0:T(8,128)(2,1)} %collective-permute-done.refs_4_), channel_id=1, source_target_pairs={{0,128},{4,132},{8,136},{12,140},{16,144},{20,148},{24,152},{28,15... | collective-permute-start | bytes 3145736 | tf_op jit(solution)/shard_map/ppermute | solution.py:73
  87.3 23.2 %collective-permute-start.13 = (bf16[128,4096]{1,0:T(8,128)(2,1)}, bf16[128,4096]{1,0:T(8,128)(2,1)}, u32[]{:S(2)}, u32[]{:S(2)}) collective-permute-start(bf16[128,4096]{1,0:T(8,128)(2,1)} %get-tuple-element.49), channel_id=1, source_target_pairs={{0,64},{4,68},{8,72},{12,76},{16,80},{20,84},{24,88},{28,92},{32,9... | collective-permute-start | bytes 3145736 | tf_op jit(solution)/shard_map/ppermute | solution.py:73
  89.4 34.9 %collective-permute-start.8 = (bf16[128,4096]{1,0:T(8,128)(2,1)}, bf16[128,4096]{1,0:T(8,128)(2,1)}, u32[]{:S(2)}, u32[]{:S(2)}) collective-permute-start(bf16[128,4096]{1,0:T(8,128)(2,1)} %collective-permute-done.7.refs_4_), channel_id=1, source_target_pairs={{0,128},{4,132},{8,136},{12,140},{16,144},{20,148},{24,152},{28,15... | collective-permute-start | bytes 3145736 | tf_op jit(solution)/shard_map/ppermute | solution.py:73
  110.5 96.3 %collective-permute-start.15 = (bf16[256,4096]{1,0:T(8,128)(2,1)}, bf16[256,4096]{1,0:T(8,128)(2,1)S(1)}, u32[]{:S(2)}, u32[]{:S(2)}) collective-permute-start(bf16[256,4096]{1,0:T(8,128)(2,1)} %broadcast_select_fusion), channel_id=1, source_target_pairs={{0,32},{4,8},{8,4},{12,16},{16,12},{20,24},{24,20},{28,124},{32,64... | collective-permute-start | bytes 6291464 | tf_op jit(solution)/shard_map/ppermute | solution.py:73
  110.8 65.1 %collective-permute-start.16 = (bf16[128,4096]{1,0:T(8,128)(2,1)}, bf16[128,4096]{1,0:T(8,128)(2,1)}, u32[]{:S(2)}, u32[]{:S(2)}) collective-permute-start(bf16[128,4096]{1,0:T(8,128)(2,1)} %collective-permute-done.13.refs_5_), channel_id=1, source_target_pairs={{0,128},{4,132},{8,136},{12,140},{16,144},{20,148},{24,152},{28,15... | collective-permute-start | bytes 3145736 | tf_op jit(solution)/shard_map/ppermute | solution.py:73
  124.4 12.7 %collective-permute-start.11 = (f32[1,256]{1,0:T(1,128)}, f32[1,256]{1,0:T(1,128)S(1)}, u32[]{:S(2)}, u32[]{:S(2)}) collective-permute-start(f32[1,256]{1,0:T(1,128)} %get-tuple-element.45), channel_id=1, source_target_pairs={{0,4},{4,0},{8,12},{12,8},{16,20},{20,16},{24,28},{28,24},{32,36},... | collective-permute-start | bytes 3080 | tf_op jit(solution)/shard_map/ppermute | solution.py:73
  126.5 13.1 %collective-permute-start.18 = (f32[8,128]{1,0:T(8,128)}, f32[8,128]{1,0:T(8,128)S(1)}, u32[]{:S(2)}, u32[]{:S(2)}) collective-permute-start(f32[8,128]{1,0:T(8,128)} %get-tuple-element.55), channel_id=1, source_target_pairs={{0,128},{4,132},{128,0},{132,4},{1,129},{5,133},{129,1},{133,5},{2... | collective-permute-start | bytes 12296 | tf_op jit(solution)/shard_map/ppermute | solution.py:403
  138.2 33.1 %collective-permute-start.10 = (f32[1,256]{1,0:T(1,128)S(1)}, f32[1,256]{1,0:T(1,128)S(1)}, u32[]{:S(2)}, u32[]{:S(2)}) collective-permute-start(f32[1,256]{1,0:T(1,128)S(1)} %copy-done.8), channel_id=1, source_target_pairs={{0,192},{4,196},{8,200},{12,204},{16,208},{20,212},{24,216},{28,22... | collective-permute-start | bytes 3080 | tf_op jit(solution)/shard_map/ppermute | solution.py:73
  140.2 33.5 %collective-permute-start.22 = (f32[8,128]{1,0:T(8,128)S(1)}, f32[8,128]{1,0:T(8,128)S(1)}, u32[]{:S(2)}, u32[]{:S(2)}) collective-permute-start(f32[8,128]{1,0:T(8,128)S(1)} %add_add_fusion.3), channel_id=1, source_target_pairs={{0,24},{8,0},{16,8},{24,16},{1,25},{9,1},{17,9},{25,17},{2,26},{10... | collective-permute-start | bytes 12296 | tf_op jit(solution)/shard_map/ppermute | solution.py:403
  155.4 18.4 %collective-permute-start.21 = (f32[8,128]{1,0:T(8,128)S(1)}, f32[8,128]{1,0:T(8,128)S(1)}, u32[]{:S(2)}, u32[]{:S(2)}) collective-permute-start(f32[8,128]{1,0:T(8,128)S(1)} %add_add_fusion.3), channel_id=1, source_target_pairs={{0,16},{8,24},{16,0},{24,8},{1,17},{9,25},{17,1},{25,9},{2,18},{10... | collective-permute-start | bytes 12296 | tf_op jit(solution)/shard_map/ppermute | solution.py:403
  173.8 19.6 %collective-permute-start.9 = (f32[1,256]{1,0:T(1,128)S(1)}, f32[1,256]{1,0:T(1,128)S(1)}, u32[]{:S(2)}, u32[]{:S(2)}) collective-permute-start(f32[1,256]{1,0:T(1,128)S(1)} %copy-done.8), channel_id=1, source_target_pairs={{0,252},{4,8},{8,4},{12,16},{16,12},{20,24},{24,20},{28,32},{32,28... | collective-permute-start | bytes 3080 | tf_op jit(solution)/shard_map/ppermute | solution.py:73
  189.5 16.1 %collective-permute-start.28 = (f32[8,128]{1,0:T(8,128)S(1)}, f32[8,128]{1,0:T(8,128)S(1)}, u32[]{:S(2)}, u32[]{:S(2)}) collective-permute-start(f32[8,128]{1,0:T(8,128)S(1)} %add_add_fusion.1), channel_id=1, source_target_pairs={{0,96},{32,0},{64,32},{96,64},{1,97},{33,1},{65,33},{97,65},{2,98}... | collective-permute-start | bytes 12296 | tf_op jit(solution)/shard_map/ppermute | solution.py:403
  189.6 16.0 %collective-permute-start.27 = (f32[8,128]{1,0:T(8,128)S(1)}, f32[8,128]{1,0:T(8,128)S(1)}, u32[]{:S(2)}, u32[]{:S(2)}) collective-permute-start(f32[8,128]{1,0:T(8,128)S(1)} %add_add_fusion.1), channel_id=1, source_target_pairs={{0,64},{32,96},{64,0},{96,32},{1,65},{33,97},{65,1},{97,33},{2,66}... | collective-permute-start | bytes 12296 | tf_op jit(solution)/shard_map/ppermute | solution.py:403
  191.0 14.5 %collective-permute-start.26 = (f32[8,128]{1,0:T(8,128)S(1)}, f32[8,128]{1,0:T(8,128)S(1)}, u32[]{:S(2)}, u32[]{:S(2)}) collective-permute-start(f32[8,128]{1,0:T(8,128)S(1)} %add_add_fusion.1), channel_id=1, source_target_pairs={{0,32},{32,64},{64,96},{96,0},{1,33},{33,65},{65,97},{97,1},{2,34}... | collective-permute-start | bytes 12296 | tf_op jit(solution)/shard_map/ppermute | solution.py:403
  (16 other events, 174.4 us)
Sparse Core Ops, SparseCore 0:
  12.2 21.8 all-gather.2
  48.4 20.9 all-gather.4
